TPU v7x, 32 devices: a whole 2x2x4 slice. The times are simulated.
32 devices in a mesh: expert: 16 (over z, x, core), fsdp: 2 (over y).
Axes of the slice: x: 2, y: 2, z: 4, core: 2. Of those that a mesh axis runs over, the one named last changes fastest.
Arguments:
- tokens: bfloat16 [512, 4096], P('expert', 'fsdp'), may hold values from -6 to 6
- expert_ids: int32 [512, 8], P('expert'), may hold values from 0 to 63, all different within a row; in each aligned block of 32 rows (0 to 31, 32 to 63, ...) at most 8 rows name the same one
- gate_up: bfloat16 [64, 2, 1536, 4096], P('expert', None, 'fsdp'), may hold values from -0.09375 to 0.09375
- hidden_grad: bfloat16 [64, 1536, 128], P('expert', 'fsdp'), may hold values from -1.5 to 1.5
Outputs:
- hidden: bfloat16 [64, 1536, 128], P('expert', 'fsdp')
- gate_up_grad: bfloat16 [64, 2, 1536, 4096], P('expert', None, 'fsdp')
- tokens_grad: bfloat16 [512, 4096], P('expert', 'fsdp')
Inputs may be any that keep to these rules, and one draw needn't show every extreme that they name: `expert_ids`: each token names 8 different experts. Among the 32 tokens of each aligned block (the tokens of one expert index) no expert is named by more than 8 tokens, and in some block one expert is named by exactly 8.
All inputs are finite; a program needn't handle non-finite values.
Results may differ from a plain program's by a relative error of at most 0.017.
Values may be sent and summed in bfloat16 or wider, within the bound.
A program may use at most 192 MiB of HBM per device.

v0:
```python
import jax
import jax.numpy as jnp
from jax import lax
from jax.sharding import PartitionSpec as P


def dispatch_table(expert_ids, all_experts, groups, capacity):
    expert_iota = jnp.arange(all_experts, dtype=jnp.int32)
    chosen = jnp.sum((expert_ids[:, :, None] == expert_iota).astype(jnp.int32), axis=1)
    before = jnp.cumsum(chosen, axis=0) - chosen
    slot_iota = jnp.arange(capacity, dtype=jnp.int32)
    placed = (chosen.T[:, None, :] == 1) & (before.T[:, None, :] == slot_iota[None, :, None])
    token_rows = expert_ids.shape[0]
    placed = placed.reshape(groups, all_experts // groups, capacity, token_rows)
    return jnp.transpose(placed, (1, 0, 2, 3))


def local(tokens, expert_ids, gate_up, hidden_grad):
    groups = lax.axis_size("expert")
    local_experts = gate_up.shape[0]
    slot_count = hidden_grad.shape[2]
    capacity = slot_count // groups
    model_width = gate_up.shape[3]
    selector = dispatch_table(expert_ids, local_experts * groups, groups, capacity)
    selector_half = selector.astype(jnp.bfloat16)
    features = lax.all_gather(tokens, "fsdp", axis=1, tiled=True)
    outgoing = jnp.einsum(
        "jgct,td->jgcd", selector_half, features, preferred_element_type=jnp.float32
    ).astype(jnp.bfloat16)
    arrived = lax.all_to_all(outgoing, "expert", split_axis=1, concat_axis=1, tiled=True)
    routed = arrived.reshape(local_experts, slot_count, model_width)
    projected = jnp.einsum("jwid,jsd->jwis", gate_up, routed, preferred_element_type=jnp.float32)
    gate_value = projected[:, 0]
    up_value = projected[:, 1]
    sigmoid_gate = 1.0 / (1.0 + jnp.exp(-gate_value))
    active = gate_value * sigmoid_gate
    hidden = (active * up_value).astype(jnp.bfloat16)
    grad_value = hidden_grad.astype(jnp.float32)
    gate_grad = (
        grad_value * up_value * sigmoid_gate * (1.0 + gate_value * (1.0 - sigmoid_gate))
    ).astype(jnp.bfloat16)
    up_grad = (grad_value * active).astype(jnp.bfloat16)
    grad_pair = jnp.stack([gate_grad, up_grad], axis=1)
    weight_grad = jnp.einsum(
        "jwis,jsd->jwid", grad_pair, routed, preferred_element_type=jnp.float32
    ).astype(jnp.bfloat16)
    summed = lax.psum_scatter(
        jnp.einsum("jwis,jwid->djs", grad_pair, gate_up, preferred_element_type=jnp.float32).astype(
            jnp.bfloat16
        ),
        "fsdp",
        scatter_dimension=0,
        tiled=True,
    ).astype(jnp.float32)
    summed = summed.reshape(summed.shape[0], local_experts, groups, capacity)
    returned = lax.all_to_all(
        summed.astype(jnp.bfloat16), "expert", split_axis=2, concat_axis=2, tiled=True
    ).astype(summed.dtype)
    token_grad = jnp.einsum(
        "jgct,djgc->td", selector.astype(jnp.float32), returned, precision=lax.Precision.HIGHEST
    ).astype(jnp.bfloat16)
    return (hidden, weight_grad, token_grad)


def solution(mesh):
    placed = (
        P("expert", "fsdp"),
        P("expert", None),
        P("expert", None, "fsdp", None),
        P("expert", "fsdp", None),
    )
    return jax.shard_map(
        local,
        mesh=mesh,
        in_specs=placed,
        out_specs=(P("expert", "fsdp", None), P("expert", None, "fsdp", None), P("expert", "fsdp")),
        check_vma=False,
    )
```

profile of v0, /device:TPU:9, one launch (start us, length us, event | category | flops | bytes accessed | tf_op | source)
XLA Modules:
  0.0 284.8 jit_solution(9027381368199624546)
XLA Ops:
  7.2 0.8 copy.44
  7.9 0.1 convert_reduce_fusion
  8.1 0.1 copy.45
  8.2 0.1 reduce_window_sum.11
  8.2 0.1 copy.47
  8.3 5.3 %all_gather.3 = bf16[32,4096]{1,0:T(8,128)(2,1)S(1)} all-gather(bf16[32,2048]{1,0:T(8,128)(2,1)} %param.4), channel_id=1, replica_groups=mesh['expert'=16,'fsdp'=2] {'fsdp'}, dimensions={1}, use_global_device_ids=true | all-gather | bytes 393216 | tf_op jit(solution)/shard_map/all_gather | solution.py:26
  13.6 1.2 convolution_convert_fusion.1
  14.9 2.3 copy.50
  17.2 0.0 copy-start.1
  17.2 7.6 %all-to-all-start = ((bf16[4,16,8,4096]{3,2,0,1:T(8,128)(2,1)}), bf16[4,16,8,4096]{3,2,0,1:T(8,128)(2,1)}, u32[]{:S(2)}, u32[]{:S(2)}) async-start(bf16[4,16,8,4096]{3,2,0,1:T(8,128)(2,1)} %copy.50), calls=%async_computation | async-start | bytes 8388608 | tf_op jit(solution)/shard_map/all_to_all | solution.py:30
  24.7 0.0 reduce-scatter.2.cloned.1.call-start
  24.8 0.0 copy-done.1
  24.8 1.2 copy.53
  26.0 89.1 %all-to-all-done = bf16[4,16,8,4096]{3,2,0,1:T(8,128)(2,1)} async-done(((bf16[4,16,8,4096]{3,2,0,1:T(8,128)(2,1)}), bf16[4,16,8,4096]{3,2,0,1:T(8,128)(2,1)}, u32[]{:S(2)}, u32[]{:S(2)}) %all-to-all-start) | async-done | bytes 4194336 | tf_op jit(solution)/shard_map/all_to_all | solution.py:30
  115.1 23.3 %fusion.14 = f32[4,2,768,128]{2,3,1,0:T(8,128)S(1)} fusion(bf16[4,2,768,4096]{3,2,1,0:T(8,128)(2,1)} %param.6, bf16[4,16,8,4096]{3,2,0,1:T(8,128)(2,1)} %all-to-all-done), kind=kOutput, calls=%fused_computation.16 | convolution fusion | flops 6442450944 | bytes 57671680 | tf_op jit(solution)/shard_map/jwid,jsd->jwis/dot_general | solution.py:32
  138.4 3.5 %fusion.24 = (bf16[4,1,768,128]{2,3,0,1:T(8,128)(2,1)}, bf16[4,1,768,128]{2,3,0,1:T(8,128)(2,1)}, bf16[4,768,128]{1,2,0:T(8,128)(2,1)}) fusion(f32[4,2,768,128]{2,3,1,0:T(8,128)S(1)} %fusion.14, bf16[4,768,128]{1,2,0:T(8,128)(2,1)} %copy.53), kind=kLoop, calls=%fused_computation.29 | loop fusion | flops 6291456 | bytes 6291456 | tf_op jit(solution)/shard_map/stack | solution.py:43
  141.9 20.8 %fusion.4 = bf16[4096,4,128]{0,2,1:T(8,128)(2,1)} fusion(bf16[4,2,768,4096]{3,2,1,0:T(8,128)(2,1)} %param.6, bf16[4,1,768,128]{2,3,0,1:T(8,128)(2,1)} %get-tuple-element.16, bf16[4,1,768,128]{2,3,0,1:T(8,128)(2,1)} %get-tuple-element.15), kind=kOutput, calls=%fused_computation.5 | convolution fusion | flops 6445334528 | bytes 56098816 | tf_op jit(solution)/shard_map/jwis,jwid->djs/dot_general | solution.py:48
  162.7 0.0 reduce-scatter.2.cloned.1.call-update
  162.7 56.1 %reduce-scatter.2.cloned.1.call-done = bf16[2048,4,128]{0,2,1:T(8,128)(2,1)} async-done(((bf16[4096,4,128]{0,2,1:T(8,128)(2,1)}), bf16[2048,4,128]{0,2,1:T(8,128)(2,1)}) %reduce-scatter.2.cloned.1.call-update) | async-done | bytes 2097168 | tf_op jit(solution)/shard_map/reduce_scatter | solution.py:47
  218.8 4.7 %copy.56 = bf16[2048,4,16,8]{0,1,3,2:T(4,128)(2,1)} copy(bf16[2048,4,16,8]{0,3,2,1:T(8,128)(2,1)} %bitcast.69) | data formatting | bytes 4194304 | tf_op jit(solution)/shard_map/convert_element_type | solution.py:57
  223.5 0.0 copy-start
  223.5 6.5 %all-to-all-start.1 = ((bf16[2048,4,16,8]{0,1,3,2:T(4,128)(2,1)}), bf16[2048,4,16,8]{0,1,3,2:T(4,128)(2,1)S(1)}, u32[]{:S(2)}, u32[]{:S(2)}) async-start(bf16[2048,4,16,8]{0,1,3,2:T(4,128)(2,1)} %copy.56), calls=%async_computation.2 | async-start | bytes 4194304 | tf_op jit(solution)/shard_map/all_to_all | solution.py:56
  230.0 0.0 copy-done
  230.0 1.2 copy.58
  231.2 22.3 %convolution_convert_fusion = bf16[4,2,768,4096]{3,2,1,0:T(8,128)(2,1)} fusion(bf16[4,16,8,4096]{3,2,0,1:T(8,128)(2,1)} %all-to-all-done, bf16[4,1,768,128]{2,3,0,1:T(8,128)(2,1)} %get-tuple-element.16, bf16[4,1,768,128]{2,3,0,1:T(8,128)(2,1)} %get-tuple-element.15), kind=kOutput, calls=%fused_computation.2 | convolution fusion | flops 6468403200 | bytes 56098816 | tf_op jit(solution)/shard_map/jwis,jsd->jwid/dot_general | solution.py:44
  253.5 22.5 %all-to-all-done.1 = bf16[2048,4,16,8]{0,1,3,2:T(4,128)(2,1)S(1)} async-done(((bf16[2048,4,16,8]{0,1,3,2:T(4,128)(2,1)}), bf16[2048,4,16,8]{0,1,3,2:T(4,128)(2,1)S(1)}, u32[]{:S(2)}, u32[]{:S(2)}) %all-to-all-start.1) | async-done | bytes 2097184 | tf_op jit(solution)/shard_map/all_to_all | solution.py:56
  276.0 1.9 fusion.12
  (5 shorter events, 0.1 us)
Async XLA Ops:
  17.2 7.6 %copy-start.1 = (bf16[4,768,128]{2,1,0:T(8,128)(2,1)S(1)}, bf16[4,768,128]{2,1,0:T(8,128)(2,1)}, u32[]{:S(2)}) copy-start(bf16[4,768,128]{2,1,0:T(8,128)(2,1)} %param.7) | copy-start | bytes 2359300
  17.2 97.9 %all-to-all-start = ((bf16[4,16,8,4096]{3,2,0,1:T(8,128)(2,1)}), bf16[4,16,8,4096]{3,2,0,1:T(8,128)(2,1)}, u32[]{:S(2)}, u32[]{:S(2)}) async-start(bf16[4,16,8,4096]{3,2,0,1:T(8,128)(2,1)} %copy.50), calls=%async_computation | async-start | bytes 8388608 | tf_op jit(solution)/shard_map/all_to_all | solution.py:30
  24.7 194.1 %reduce-scatter.2.cloned.1.call-start = ((), (), s32[]{:S(2)}) async-start(), calls=%async_computation.3 | async-start | bytes 6291456 | tf_op jit(solution)/shard_map/reduce_scatter | solution.py:47
  223.5 6.5 %copy-start = (bf16[4,768,128]{1,2,0:T(8,128)(2,1)S(1)}, bf16[4,768,128]{1,2,0:T(8,128)(2,1)}, u32[]{:S(2)}) copy-start(bf16[4,768,128]{1,2,0:T(8,128)(2,1)} %get-tuple-element.17) | copy-start | bytes 2359300
  223.5 52.5 %all-to-all-start.1 = ((bf16[2048,4,16,8]{0,1,3,2:T(4,128)(2,1)}), bf16[2048,4,16,8]{0,1,3,2:T(4,128)(2,1)S(1)}, u32[]{:S(2)}, u32[]{:S(2)}) async-start(bf16[2048,4,16,8]{0,1,3,2:T(4,128)(2,1)} %copy.56), calls=%async_computation.2 | async-start | bytes 4194304 | tf_op jit(solution)/shard_map/all_to_all | solution.py:56
Sparse Core Ops, SparseCore 0:
  162.9 55.9 reduce-scatter.1
where the time goes:
time: 287 us; the launch traced here: 285 us
  waiting for transfers between devices  168 us (59%)
  matrix products  69.6 us (24%)
  starting transfers between devices  14.1 us (5%)
  between operations  14.1 us (5%)
  local copies, waits for them, and re-layouts  10.3 us (4%)
  blocking collectives  5.25 us (2%)
  other arithmetic  3.72 us (1%)
    all_to_all x1, waiting for transfers between devices, local(): lax.all_to_all(outgoing, 'expert', split_axis=1, concat_axis=1, tiled=True)  89.1 us
    reduce_scatter x1, waiting for transfers between devices, local(): lax.psum_scatter(jnp.einsum('jwis,jwid->djs', grad_pair, gate_up, preferr...  56.1 us
    dot_general x1, matrix products, local(): jnp.einsum('jwid,jsd->jwis', gate_up, routed, preferred_element_type=jnp....  23.3 us
    all_to_all x1, waiting for transfers between devices, local(): lax.all_to_all(summed.astype(jnp.bfloat16), 'expert', split_axis=2, conca...  22.5 us
    dot_general x1, matrix products, local(): jnp.einsum('jwis,jsd->jwid', grad_pair, routed, preferred_element_type=jn...  22.3 us
    dot_general x1, matrix products, local(): jnp.einsum('jwis,jwid->djs', grad_pair, gate_up, preferred_element_type=j...  20.8 us
    all_to_all x1, starting transfers between devices, local(): lax.all_to_all(outgoing, 'expert', split_axis=1, concat_axis=1, tiled=True)  7.59 us
    all_to_all x1, starting transfers between devices, local(): lax.all_to_all(summed.astype(jnp.bfloat16), 'expert', split_axis=2, conca...  6.5 us
  transfers between devices with their start and end apart: 3, of which 3 were waited for; matrix products, arithmetic and copies ran while one was open for 9% of the time, Pallas kernels for 0%

commit v1 on v0

v1 whole, which is shorter than its diff:
```python
import jax
import jax.numpy as jnp
from jax import lax
from jax.sharding import PartitionSpec as P


def selector_of(ids, first, local_experts, groups, capacity):
    rows = ids.shape[0] // groups
    mine = first + jnp.arange(local_experts, dtype=jnp.int32)
    chosen = jnp.sum((ids[:, :, None] == mine).astype(jnp.int32), axis=1)
    chosen = chosen.reshape(groups, rows, local_experts)
    before = jnp.cumsum(chosen, axis=1) - chosen
    group = jnp.arange(groups, dtype=jnp.int32)[:, None, None]
    slot = jnp.where(chosen == 1, group * capacity + before, -1)
    slot = slot.reshape(groups * rows, local_experts)
    slots = jnp.arange(groups * capacity, dtype=jnp.int32)
    return (slot.T[:, None, :] == slots[None, :, None]).astype(jnp.bfloat16)


def local(tokens, expert_ids, gate_up, hidden_grad):
    groups = lax.axis_size("expert")
    local_experts, _, units, model_width = gate_up.shape
    slot_count = hidden_grad.shape[2]
    capacity = slot_count // groups
    ids = lax.all_gather(expert_ids, "expert", axis=0, tiled=True)
    selector = selector_of(
        ids, lax.axis_index("expert") * local_experts, local_experts, groups, capacity
    )
    features = lax.all_gather(tokens, "fsdp", axis=1, tiled=True)
    features = lax.all_gather(features, "expert", axis=0, tiled=True)
    routed = jnp.einsum(
        "jst,td->jsd", selector, features, preferred_element_type=jnp.float32
    ).astype(jnp.bfloat16)
    projected = jnp.einsum("jwid,jsd->jwis", gate_up, routed, preferred_element_type=jnp.float32)
    gate_value = projected[:, 0]
    up_value = projected[:, 1]
    sigmoid_gate = 1.0 / (1.0 + jnp.exp(-gate_value))
    active = gate_value * sigmoid_gate
    hidden = (active * up_value).astype(jnp.bfloat16)
    grad_value = hidden_grad.astype(jnp.float32)
    gate_grad = (
        grad_value * up_value * sigmoid_gate * (1.0 + gate_value * (1.0 - sigmoid_gate))
    ).astype(jnp.bfloat16)
    up_grad = (grad_value * active).astype(jnp.bfloat16)
    grad_pair = jnp.stack([gate_grad, up_grad], axis=1)
    part = jnp.einsum(
        "jwis,jwid->jsd", grad_pair, gate_up, preferred_element_type=jnp.float32
    ).astype(jnp.bfloat16)
    partial = jnp.einsum(
        "jst,jsd->td", selector, part, preferred_element_type=jnp.float32
    ).astype(jnp.bfloat16)
    summed = lax.psum_scatter(partial, "expert", scatter_dimension=0, tiled=True)
    token_grad = lax.psum_scatter(summed, "fsdp", scatter_dimension=1, tiled=True)
    weight_grad = jnp.einsum(
        "jwis,jsd->jwid", grad_pair, routed, preferred_element_type=jnp.float32
    ).astype(jnp.bfloat16)
    return (hidden, weight_grad, token_grad)


def solution(mesh):
    placed = (
        P("expert", "fsdp"),
        P("expert", None),
        P("expert", None, "fsdp", None),
        P("expert", "fsdp", None),
    )
    return jax.shard_map(
        local,
        mesh=mesh,
        in_specs=placed,
        out_specs=(P("expert", "fsdp", None), P("expert", None, "fsdp", None), P("expert", "fsdp")),
        check_vma=False,
    )
```

time: 287 us -> 223 us (0.78)
  waiting for transfers between devices: 168 us -> 94.8 us
  blocking collectives: 5.25 us -> 27.5 us
  starting transfers between devices: 14.1 us -> 0.3 us
  local copies, waits for them, and re-layouts: 10.3 us -> 4.27 us
  matrix products: 69.6 us -> 73.3 us
    all_to_all x2 -> x0, waiting for transfers between devices: 112 us -> none  [the longest x1 89.1 us: local(): lax.all_to_all(outgoing, 'expert', split_axis=1, concat_axis=1, tiled=True)]
    all_gather x0 -> x1, waiting for transfers between devices: none -> 26.4 us  [local(): features = lax.all_gather(features, 'expert', axis=0, tiled=True)]
    all_gather x0 -> x1, blocking collectives: none -> 20.5 us  [local(): ids = lax.all_gather(expert_ids, 'expert', axis=0, tiled=True)]
    all_to_all x2 -> x0, starting transfers between devices: 14.1 us -> none  [the longest x1 7.59 us: local(): lax.all_to_all(outgoing, 'expert', split_axis=1, concat_axis=1, tiled=True)]
    reduce_scatter x1 -> x2, waiting for transfers between devices: 56.1 us -> 68.3 us  [the longest x1 68.3 us: local(): lax.psum_scatter(partial, 'expert', scatter_dimension=0, tiled=True)]
    convert_element_type x2 -> x0, local copies, waits for them, and re-layouts: 6.99 us -> none  [the longest x1 4.7 us: local(): summed.astype(jnp.bfloat16)]
    dot_general x3 -> x2, matrix products: 24 us -> 28.3 us  [the longest x1 22 us: local(): jnp.einsum('jst,jsd->td', selector, part, preferred_element_type=jnp.floa...]
  transfers between devices with their start and end apart: 3 -> 3, of which waited for: 3 -> 2; matrix products, arithmetic and copies ran while one was open for 9% -> 13% of each run, Pallas kernels for 0% -> 0%
where the time goes in v1:
time: 223 us; the launch traced here: 219 us
  waiting for transfers between devices  94.8 us (43%)
  matrix products  73.3 us (33%)
  blocking collectives  27.5 us (12%)
  between operations  13.8 us (6%)
  other arithmetic  5.42 us (2%)
  local copies, waits for them, and re-layouts  4.27 us (2%)
    reduce_scatter x1, waiting for transfers between devices, local(): lax.psum_scatter(partial, 'expert', scatter_dimension=0, tiled=True)  68.3 us
    all_gather x1, waiting for transfers between devices, local(): features = lax.all_gather(features, 'expert', axis=0, tiled=True)  26.4 us
    dot_general x1, matrix products, local(): jnp.einsum('jwis,jsd->jwid', grad_pair, routed, preferred_element_type=jn...  22.9 us
    dot_general x1, matrix products, local(): jnp.einsum('jst,jsd->td', selector, part, preferred_element_type=jnp.floa...  22 us
    dot_general x1, matrix products, local(): jnp.einsum('jwid,jsd->jwis', gate_up, routed, preferred_element_type=jnp....  22 us
    all_gather x1, blocking collectives, local(): ids = lax.all_gather(expert_ids, 'expert', axis=0, tiled=True)  20.5 us
    all_gather x1, blocking collectives, local(): features = lax.all_gather(tokens, 'fsdp', axis=1, tiled=True)  6.98 us
    dot_general x1, matrix products, local(): jnp.einsum('jst,td->jsd', selector, features, preferred_element_type=jnp....  6.29 us
  transfers between devices with their start and end apart: 3, of which 2 were waited for; matrix products, arithmetic and copies ran while one was open for 13% of the time, Pallas kernels for 0%

profile of v1, /device:TPU:9, one launch (start us, length us, event | category | flops | bytes accessed | tf_op | source)
XLA Modules:
  0.0 219.4 jit_solution(12228288335410436556)
XLA Ops:
  7.2 0.0 all-gather.3.cloned.1.call-start
  7.2 7.0 %all_gather.10 = bf16[32,4096]{1,0:T(8,128)(2,1)} all-gather(bf16[32,2048]{1,0:T(8,128)(2,1)} %param.4), channel_id=1, replica_groups=mesh['expert'=16,'fsdp'=2] {'fsdp'}, dimensions={1}, use_global_device_ids=true | all-gather | bytes 393216 | tf_op jit(solution)/shard_map/all_gather | solution.py:29
  14.2 0.0 all-gather.3.cloned.1.call-update
  14.2 0.0 reduce-scatter.3.cloned.1.call-start
  14.3 20.5 %all-gather = s32[16,32,8]{1,2,0:T(8,128)S(1)} all-gather(s32[1,32,8]{1,2,0:T(8,128)} %bitcast.55), channel_id=1, replica_groups=mesh['expert'=16,'fsdp'=2] {'expert'}, dimensions={0}, use_global_device_ids=true | all-gather | bytes 17408 | tf_op jit(solution)/shard_map/all_gather | solution.py:25
  34.8 0.1 reshape.25
  34.9 0.1 convert_reduce_fusion
  35.0 0.1 reshape.23
  35.1 0.2 copy.32
  35.3 1.9 fusion.18
  37.2 0.2 copy.33
  37.3 0.1 reduce_window_sum.14
  37.4 0.1 add.35
  37.5 0.1 add.36
  37.6 2.3 %copy.36 = bf16[4,768,128]{1,2,0:T(8,128)(2,1)} copy(bf16[4,768,128]{2,1,0:T(8,128)(2,1)} %param.7) | data formatting | bytes 1572864 | tf_op args[3]
  39.9 26.4 %all-gather.3.cloned.1.call-done = bf16[512,4096]{1,0:T(8,128)(2,1)} async-done(((bf16[32,4096]{1,0:T(8,128)(2,1)}), bf16[512,4096]{1,0:T(8,128)(2,1)}) %all-gather.3.cloned.1.call-update) | async-done | bytes 4194320 | tf_op jit(solution)/shard_map/all_gather | solution.py:30
  66.3 6.3 %fusion.4 = bf16[4,128,4096,1]{2,1,3,0:T(8,128)(2,1)} fusion(bf16[512,4096]{1,0:T(8,128)(2,1)} %all-gather.3.cloned.1.call-done, s32[4,512]{1,0:T(4,128)S(1)} %select_bitcast_fusion), kind=kOutput, calls=%fused_computation.6 | convolution fusion | flops 2149842944 | bytes 8396800 | tf_op jit(solution)/shard_map/jst,td->jsd/dot_general | solution.py:31
  72.6 22.0 %convolution_bitcast_fusion = f32[4,2,768,128]{2,3,1,0:T(8,128)S(1)} fusion(bf16[4,128,4096,1]{2,1,3,0:T(8,128)(2,1)} %fusion.4, bf16[4,2,768,4096]{3,2,1,0:T(8,128)(2,1)} %param.6), kind=kOutput, calls=%fused_computation.10 | convolution fusion | flops 6442450944 | bytes 57671680 | tf_op jit(solution)/shard_map/jwid,jsd->jwis/dot_general | solution.py:34
  94.6 3.4 %fusion.15 = (bf16[4,1,768,128]{2,3,0,1:T(8,128)(2,1)}, bf16[4,1,768,128]{2,3,0,1:T(8,128)(2,1)}, bf16[4,768,128]{1,2,0:T(8,128)(2,1)}) fusion(f32[4,2,768,128]{2,3,1,0:T(8,128)S(1)} %convolution_bitcast_fusion, bf16[4,768,128]{1,2,0:T(8,128)(2,1)} %copy.36), kind=kLoop, calls=%fused_computation.24 | loop fusion | flops 6291456 | bytes 6291456 | tf_op jit(solution)/shard_map/stack | solution.py:45
  98.1 22.0 %bitcast_convert_fusion = bf16[512,4096]{1,0:T(8,128)(2,1)} fusion(bf16[4,2,768,4096]{3,2,1,0:T(8,128)(2,1)} %param.6, s32[4,512]{1,0:T(4,128)S(1)} %select_bitcast_fusion, bf16[4,1,768,128]{2,3,0,1:T(8,128)(2,1)} %get-tuple-element.16, bf16[4,1,768,128]{2,3,0,1:T(8,128)(2,1)} %get-tuple-element.15), kind=kOutput, calls=%fused_computation.3 | convolution fusion | flops 8595177472 | bytes 56107008 | tf_op jit(solution)/shard_map/jst,jsd->td/dot_general | solution.py:49
  120.1 0.0 copy-start.1
  120.1 0.0 copy-start.2
  120.1 0.0 reduce-scatter.3.cloned.1.call-update
  120.1 0.2 reduce-scatter.5.cloned.1.call-start
  120.4 68.3 %reduce-scatter.3.cloned.1.call-done = bf16[32,4096]{1,0:T(8,128)(2,1)} async-done(((bf16[512,4096]{1,0:T(8,128)(2,1)}), bf16[32,4096]{1,0:T(8,128)(2,1)}) %reduce-scatter.3.cloned.1.call-update) | async-done | bytes 262160 | tf_op jit(solution)/shard_map/reduce_scatter | solution.py:52
  188.7 0.0 reduce-scatter.5.cloned.1.call-update
  188.7 0.0 copy-done.1
  188.8 0.0 copy-done.2
  188.8 0.0 copy-start
  188.8 22.9 %convolution_convert_fusion = bf16[4,2,768,4096]{3,2,1,0:T(8,128)(2,1)} fusion(bf16[4,128,4096,1]{2,1,3,0:T(8,128)(2,1)} %fusion.4, bf16[4,1,768,128]{2,3,0,1:T(8,128)(2,1)S(1)} %copy-done.2, bf16[4,1,768,128]{2,3,0,1:T(8,128)(2,1)S(1)} %copy-done.1), kind=kOutput, calls=%fused_computation.2 | convolution fusion | flops 6468403200 | bytes 56098816 | tf_op jit(solution)/shard_map/jwis,jsd->jwid/dot_general | solution.py:54
  211.7 0.0 copy-done
  211.7 1.2 copy.39
  (5 shorter events, 0.0 us)
Async XLA Ops:
  7.2 59.2 %all-gather.3.cloned.1.call-start = ((), (), s32[]{:S(2)}) async-start(), calls=%async_computation.2 | async-start | bytes 4456448 | tf_op jit(solution)/shard_map/all_gather | solution.py:30
  14.2 174.5 %reduce-scatter.3.cloned.1.call-start = ((), (), s32[]{:S(2)}) async-start(), calls=%async_computation.3 | async-start | bytes 4456448 | tf_op jit(solution)/shard_map/reduce_scatter | solution.py:52
  120.1 68.6 %copy-start.1 = (bf16[4,1,768,128]{2,3,0,1:T(8,128)(2,1)S(1)}, bf16[4,1,768,128]{2,3,0,1:T(8,128)(2,1)}, u32[]{:S(2)}) copy-start(bf16[4,1,768,128]{2,3,0,1:T(8,128)(2,1)} %get-tuple-element.15) | copy-start | bytes 2359300
  120.1 68.6 %copy-start.2 = (bf16[4,1,768,128]{2,3,0,1:T(8,128)(2,1)S(1)}, bf16[4,1,768,128]{2,3,0,1:T(8,128)(2,1)}, u32[]{:S(2)}) copy-start(bf16[4,1,768,128]{2,3,0,1:T(8,128)(2,1)} %get-tuple-element.16) | copy-start | bytes 2359300
  120.1 92.7 %reduce-scatter.5.cloned.1.call-start = ((), (), s32[]{:S(2)}) async-start(), calls=%async_computation.4 | async-start | bytes 393216 | tf_op jit(solution)/shard_map/reduce_scatter | solution.py:53
  188.8 22.9 %copy-start = (bf16[4,768,128]{1,2,0:T(8,128)(2,1)S(1)}, bf16[4,768,128]{1,2,0:T(8,128)(2,1)}, u32[]{:S(2)}) copy-start(bf16[4,768,128]{1,2,0:T(8,128)(2,1)} %get-tuple-element.17) | copy-start | bytes 2359300
Sparse Core Ops, SparseCore 0:
  14.3 51.9 all-gather.2
  120.3 68.4 reduce-scatter.2
  191.6 12.6 reduce-scatter.4

commit v2 on v1

--- a/solution.py
+++ b/solution.py
@@ -1,7 +1,357 @@
+import functools
+
 import jax
 import jax.numpy as jnp
 from jax import lax
+from jax.experimental import pallas as pl
+from jax.experimental.pallas import tpu as pltpu
 from jax.sharding import PartitionSpec as P
+
+MIB = 2**20
+MESH = pl.DeviceIdType.MESH
+
+
+class Place:
+    def __init__(self, groups):
+        self.depth = groups // 4
+        index = lax.axis_index("expert")
+        self.core = lax.rem(index, 2)
+        self.x = lax.rem(lax.div(index, 2), 2)
+        self.z = lax.div(index, 4)
+        self.y = lax.axis_index("fsdp")
+
+    def along(self, step):
+        return lax.rem(self.z + step + self.depth, self.depth)
+
+    def expert(self, z, x, core):
+        return (z * 2 + x) * 2 + core
+
+    def device(self, z=None, x=None, y=None, core=None):
+        z = self.z if z is None else z
+        x = self.x if x is None else x
+        core = self.core if core is None else core
+        return (self.expert(z, x, core), self.y if y is None else y)
+
+    def greet(self):
+        barrier = pltpu.get_barrier_semaphore()
+        peers = [self.device(z=self.along(k)) for k in range(1, self.depth)]
+        peers += [self.device(x=1 - self.x), self.device(y=1 - self.y)]
+        peers += [self.device(core=1 - self.core)]
+        for peer in peers:
+            pl.semaphore_signal(barrier, inc=1, device_id=peer, device_id_type=MESH)
+        pl.semaphore_wait(barrier, len(peers))
+
+
+def remote(source, target, sends, recvs, at, device):
+    copy = pltpu.make_async_remote_copy(
+        src_ref=source,
+        dst_ref=target,
+        send_sem=sends.at[at],
+        recv_sem=recvs.at[at],
+        device_id=device,
+        device_id_type=MESH,
+    )
+    return copy
+
+
+def gather_kernel(groups, own, full, z_send, z_recv, p_send, p_recv, q_send, q_recv, c_send, c_recv, own_sem):
+    me = Place(groups)
+    depth = me.depth
+    me.greet()
+    other = me.device(core=1 - me.core)
+    partner = [me.device(x=1 - me.x), me.device(y=1 - me.y)]
+    started = []
+
+    def slab(h, k, kind):
+        far_x = kind in ((1, 3) if h == 0 else (2, 3))
+        far_y = kind in ((2, 3) if h == 0 else (1, 3))
+        x = 1 - me.x if far_x else me.x
+        y = 1 - me.y if far_y else me.y
+        return full.at[y, me.expert(me.along(-k), x, me.core), h]
+
+    def hand_on(h, k, kind, source):
+        target = slab(h, k, kind)
+        first, second = (partner[0], partner[1]) if h == 0 else (partner[1], partner[0])
+        copies = []
+        if kind == 0:
+            copies.append(remote(source, target, p_send, p_recv, (h, k), first))
+        if kind in (0, 1):
+            copies.append(remote(source, target, q_send, q_recv, (h, k, kind), second))
+        copies.append(remote(source, target, c_send, c_recv, (h, k, kind), other))
+        for copy in copies:
+            copy.start()
+            started.append(copy)
+
+    def arrived(sems, at, h, k, kind):
+        target = slab(h, k, kind)
+        remote(target, target, sems, sems, at, other).wait_recv()
+
+    mine = pltpu.make_async_copy(own, full.at[me.y, lax.axis_index("expert")], own_sem)
+    mine.start()
+    for k in range(1, depth):
+        for h in range(2):
+            copy = remote(
+                own.at[h], slab(h, 0, 0), z_send, z_recv, (h, k), me.device(z=me.along(k))
+            )
+            copy.start()
+            started.append(copy)
+    for h in range(2):
+        hand_on(h, 0, 0, own.at[h])
+    for k in range(depth):
+        if k > 0:
+            for h in range(2):
+                arrived(z_recv, (h, k), h, k, 0)
+                hand_on(h, k, 0, slab(h, k, 0))
+        for h in range(2):
+            arrived(p_recv, (h, k), h, k, 1)
+            hand_on(h, k, 1, slab(h, k, 1))
+    for k in range(depth):
+        for kind in (2, 3):
+            for h in range(2):
+                arrived(q_recv, (h, k, kind - 2), h, k, kind)
+                hand_on(h, k, kind, slab(h, k, kind))
+    for k in range(depth):
+        for kind in range(4):
+            for h in range(2):
+                far = full.at[me.y, me.expert(me.along(-k), me.x, 1 - me.core), h]
+                remote(far, far, c_send, c_recv, (h, k, kind), other).wait_recv()
+    for copy in started:
+        copy.wait_send()
+    mine.wait()
+
+
+def gather_tokens(own, groups, fsdp):
+    depth = groups // 4
+    dma = pltpu.SemaphoreType.DMA
+    return pl.pallas_call(
+        functools.partial(gather_kernel, groups),
+        out_shape=jax.ShapeDtypeStruct((fsdp, groups) + own.shape, own.dtype),
+        in_specs=[pl.BlockSpec(memory_space=pl.ANY)],
+        out_specs=pl.BlockSpec(memory_space=pl.ANY),
+        scratch_shapes=[
+            dma((2, depth)),
+            dma((2, depth)),
+            dma((2, depth)),
+            dma((2, depth)),
+            dma((2, depth, 2)),
+            dma((2, depth, 2)),
+            dma((2, depth, 4)),
+            dma((2, depth, 4)),
+            dma,
+        ],
+        compiler_params=pltpu.CompilerParams(collective_id=0, has_side_effects=True),
+        name="gather_tokens",
+    )(own)
+
+
+def add_into(target, term):
+    total = target[...].astype(jnp.float32) + term[...].astype(jnp.float32)
+    target[...] = total.astype(target.dtype)
+
+
+def scatter_kernel(groups, part, out, one, two, three, four, s1, r1, s2, r2, s3, r3, s4, r4):
+    me = Place(groups)
+    depth = me.depth
+    me.greet()
+    other = me.device(core=1 - me.core)
+    x_peer, y_peer = me.device(x=1 - me.x), me.device(y=1 - me.y)
+    started = []
+    order = list(range(1, depth)) + [0]
+
+    def send(*what):
+        copy = remote(*what)
+        copy.start()
+        started.append(copy)
+
+    def arrived(target, sems, at):
+        remote(target, target, sems, sems, at, other).wait_recv()
+
+    def side(i, mine):
+        return 1 - mine if i == 0 else mine
+
+    for k in order:
+        for i, j in ((0, 0), (0, 1), (1, 0), (1, 1)):
+            block = me.expert(me.along(k), side(j, me.x), 1 - me.core)
+            source = part.at[side(i, me.y), block]
+            send(source, one.at[k, i, j], s1, r1, (k, i, j), other)
+    for k in order:
+        for i, j in ((0, 0), (0, 1), (1, 0), (1, 1)):
+            arrived(one.at[k, i, j], r1, (k, i, j))
+            block = me.expert(me.along(k), side(j, me.x), me.core)
+            add_into(one.at[k, i, j], part.at[side(i, me.y), block])
+            if i == 0:
+                send(one.at[k, 0, j, 0], two.at[0, k, j], s2, r2, (0, k, j), y_peer)
+            if j == 0:
+                send(one.at[k, i, 0, 1], two.at[1, k, i], s2, r2, (1, k, i), x_peer)
+    for k in order:
+        for j in range(2):
+            arrived(two.at[0, k, j], r2, (0, k, j))
+            add_into(two.at[0, k, j], one.at[k, 1, j, 0])
+            arrived(two.at[1, k, j], r2, (1, k, j))
+            add_into(two.at[1, k, j], one.at[k, j, 1, 1])
+            if j == 0:
+                send(two.at[0, k, 0], three.at[0, k], s3, r3, (0, k), x_peer)
+                send(two.at[1, k, 0], three.at[1, k], s3, r3, (1, k), y_peer)
+    for k in order:
+        for h in range(2):
+            arrived(three.at[h, k], r3, (h, k))
+            add_into(three.at[h, k], two.at[h, k, 1])
+            if k > 0:
+                send(three.at[h, k], four.at[h, k], s4, r4, (h, k), me.device(z=me.along(k)))
+    for h in range(2):
+        total = three[h, 0].astype(jnp.float32)
+        for k in range(1, depth):
+            arrived(four.at[h, k], r4, (h, k))
+            total = total + four[h, k].astype(jnp.float32)
+        out[h] = total.astype(out.dtype)
+    for copy in started:
+        copy.wait_send()
+
+
+def scatter_sum(part):
+    _, groups, halves, rows, width = part.shape
+    depth = groups // 4
+    dma = pltpu.SemaphoreType.DMA
+    vmem = lambda *lead: pltpu.VMEM(lead + (rows, width), part.dtype)
+    return pl.pallas_call(
+        functools.partial(scatter_kernel, groups),
+        out_shape=jax.ShapeDtypeStruct((halves, rows, width), part.dtype),
+        in_specs=[pl.BlockSpec(memory_space=pltpu.VMEM)],
+        out_specs=pl.BlockSpec(memory_space=pltpu.VMEM),
+        scratch_shapes=[
+            vmem(depth, 2, 2, 2),
+            vmem(2, depth, 2),
+            vmem(2, depth),
+            vmem(2, depth),
+            dma((depth, 2, 2)),
+            dma((depth, 2, 2)),
+            dma((2, depth, 2)),
+            dma((2, depth, 2)),
+            dma((2, depth)),
+            dma((2, depth)),
+            dma((2, depth)),
+            dma((2, depth)),
+        ],
+        compiler_params=pltpu.CompilerParams(
+            collective_id=1, has_side_effects=True, vmem_limit_bytes=24 * MIB
+        ),
+        name="scatter_sum",
+    )(part)
+
+
+def mixed_kernel(
+    features, chosen, chosen_back, weights, grad, hidden, weight_grad, summed, routed, parts, pair, turned
+):
+    expert, turn = pl.program_id(0), pl.program_id(1)
+    sides, _, half = features.shape
+    units, slots = pair.shape[1:]
+    width = routed.shape[1]
+    half_width = summed.shape[2]
+    tile = 512 if half_width % 512 == 0 else 128
+    rows = 256 if units % 256 == 0 else 16
+    f32 = jnp.float32
+
+    @pl.when(turn == 0)
+    def _():
+        @pl.loop(0, half_width // tile)
+        def _(n):
+            at = pl.ds(pl.multiple_of(n * tile, tile), tile)
+            for side in range(sides):
+                to = pl.ds(pl.multiple_of(side * half_width + n * tile, tile), tile)
+                routed[:, to] = jnp.dot(
+                    chosen[0], features[side, :, at], preferred_element_type=f32
+                ).astype(routed.dtype)
+
+        @pl.loop(0, units // rows)
+        def _(n):
+            at = pl.ds(pl.multiple_of(n * rows, rows), rows)
+            contract = (((1,), (1,)), ((), ()))
+            gate = lax.dot_general(
+                weights[0, 0, at, :], routed[...], contract, preferred_element_type=f32
+            )
+            up = lax.dot_general(
+                weights[0, 1, at, :], routed[...], contract, preferred_element_type=f32
+            )
+            sigmoid = 1.0 / (1.0 + jnp.exp(-gate))
+            active = gate * sigmoid
+            hidden[0, at, :] = (active * up).astype(hidden.dtype)
+            slope = grad[0, at, :].astype(f32)
+            pair[0, at, :] = (slope * up * sigmoid * (1.0 + gate * (1.0 - sigmoid))).astype(pair.dtype)
+            pair[1, at, :] = (slope * active).astype(pair.dtype)
+
+    @pl.loop(0, width // tile)
+    def _(n):
+        at = pl.ds(pl.multiple_of(n * tile, tile), tile)
+        weight_grad[0, 0, :, at] = jnp.dot(
+            pair[turn], routed[:, at], preferred_element_type=f32
+        ).astype(weight_grad.dtype)
+
+    @pl.when(turn == 1)
+    def _():
+        turned[0] = pair[0].T
+        turned[1] = pair[1].T
+
+        @pl.loop(0, width // tile)
+        def _(n):
+            at = pl.ds(pl.multiple_of(n * tile, tile), tile)
+            total = jnp.dot(turned[0], weights[0, 0, :, at], preferred_element_type=f32)
+            total += jnp.dot(turned[1], weights[0, 1, :, at], preferred_element_type=f32)
+            parts[pl.ds(pl.multiple_of(expert * slots, slots), slots), at] = total.astype(parts.dtype)
+
+    @pl.when((turn == 1) & (expert == pl.num_programs(0) - 1))
+    def _():
+        @pl.loop(0, half_width // tile)
+        def _(n):
+            at = pl.ds(pl.multiple_of(n * tile, tile), tile)
+            for side in range(sides):
+                come = pl.ds(pl.multiple_of(side * half_width + n * tile, tile), tile)
+                summed[side, :, at] = jnp.dot(
+                    chosen_back[...], parts[:, come], preferred_element_type=f32
+                ).astype(summed.dtype)
+
+
+def mixed(features, selector, gate_up, hidden_grad, half_width):
+    experts, _, units, width = gate_up.shape
+    slots = hidden_grad.shape[2]
+    sides, tokens, _ = features.shape
+    back = jnp.transpose(selector.reshape(experts * slots, tokens))
+    bf16 = gate_up.dtype
+    flops = 2 * experts * units * width * slots * 6
+    whole = pl.BlockSpec(memory_space=pltpu.VMEM)
+    return pl.pallas_call(
+        mixed_kernel,
+        grid=(experts, 2),
+        out_shape=(
+            jax.ShapeDtypeStruct(hidden_grad.shape, bf16),
+            jax.ShapeDtypeStruct(gate_up.shape, bf16),
+            jax.ShapeDtypeStruct((sides, tokens, half_width), bf16),
+        ),
+        in_specs=[
+            whole,
+            pl.BlockSpec((1, slots, tokens), lambda j, p: (j, 0, 0)),
+            whole,
+            pl.BlockSpec((1, 2, units, width), lambda j, p: (j, 0, 0, 0)),
+            pl.BlockSpec((1, units, slots), lambda j, p: (j, 0, 0)),
+        ],
+        out_specs=(
+            pl.BlockSpec((1, units, slots), lambda j, p: (j, 0, 0)),
+            pl.BlockSpec((1, 1, units, width), lambda j, p: (j, p, 0, 0)),
+            whole,
+        ),
+        scratch_shapes=[
+            pltpu.VMEM((slots, width), bf16),
+            pltpu.VMEM((experts * slots, width), bf16),
+            pltpu.VMEM((2, units, slots), bf16),
+            pltpu.VMEM((2, slots, units), bf16),
+        ],
+        compiler_params=pltpu.CompilerParams(
+            dimension_semantics=("arbitrary", "arbitrary"), vmem_limit_bytes=60 * MIB
+        ),
+        cost_estimate=pl.CostEstimate(
+            flops=flops, bytes_accessed=4 * gate_up.size, transcendentals=experts * units * slots
+        ),
+        name="expert_pass",
+    )(features, selector, back, gate_up, hidden_grad)
 
 
 def selector_of(ids, first, local_experts, groups, capacity):
@@ -17,7 +367,7 @@
     return (slot.T[:, None, :] == slots[None, :, None]).astype(jnp.bfloat16)
 
 
-def local(tokens, expert_ids, gate_up, hidden_grad):
+def local_plain(tokens, expert_ids, gate_up, hidden_grad):
     groups = lax.axis_size("expert")
     local_experts, _, units, model_width = gate_up.shape
     slot_count = hidden_grad.shape[2]
@@ -57,6 +407,36 @@
     return (hidden, weight_grad, token_grad)
 
 
+def local(tokens, expert_ids, gate_up, hidden_grad):
+    groups, fsdp = lax.axis_size("expert"), lax.axis_size("fsdp")
+    local_experts = gate_up.shape[0]
+    capacity = hidden_grad.shape[2] // groups
+    rows, width = tokens.shape
+    listing = jnp.pad(expert_ids.astype(tokens.dtype), ((0, 0), (0, 128 - expert_ids.shape[1])))
+    own = jnp.concatenate([tokens, listing], axis=1).reshape(2, rows // 2, width + 128)
+    full = gather_tokens(own, groups, fsdp).reshape(fsdp, groups * rows, width + 128)
+    ids = full[0, :, width : width + expert_ids.shape[1]].astype(jnp.int32)
+    selector = selector_of(
+        ids, lax.axis_index("expert") * local_experts, local_experts, groups, capacity
+    )
+    hidden, weight_grad, partial = mixed(full, selector, gate_up, hidden_grad, width)
+    token_grad = scatter_sum(partial.reshape(fsdp, groups, 2, rows // 2, width))
+    return (hidden, weight_grad, token_grad.reshape(rows, width))
+
+
+def fits(mesh, gate_up_shape, ids_shape, tokens_shape):
+    groups, fsdp = mesh.shape["expert"], mesh.shape["fsdp"]
+    rows = tokens_shape[0] // groups
+    return (
+        groups % 4 == 0
+        and fsdp == 2
+        and rows % 32 == 0
+        and (tokens_shape[1] // fsdp) % 128 == 0
+        and gate_up_shape[0] <= 256
+        and ids_shape[1] <= 128
+    )
+
+
 def solution(mesh):
     placed = (
         P("expert", "fsdp"),
@@ -64,10 +444,16 @@
         P("expert", None, "fsdp", None),
         P("expert", "fsdp", None),
     )
-    return jax.shard_map(
-        local,
-        mesh=mesh,
-        in_specs=placed,
-        out_specs=(P("expert", "fsdp", None), P("expert", None, "fsdp", None), P("expert", "fsdp")),
-        check_vma=False,
-    )
+    results = (P("expert", "fsdp", None), P("expert", None, "fsdp", None), P("expert", "fsdp"))
+
+    def run(tokens, expert_ids, gate_up, hidden_grad):
+        kernels = fits(mesh, gate_up.shape, expert_ids.shape, tokens.shape)
+        return jax.shard_map(
+            local if kernels else local_plain,
+            mesh=mesh,
+            in_specs=placed,
+            out_specs=results,
+            check_vma=False,
+        )(tokens, expert_ids, gate_up, hidden_grad)
+
+    return run

time: 223 us -> 151 us (0.68); the launches traced: 219 us -> 150 us
  Pallas kernels: 0 us -> 138 us
  waiting for transfers between devices: 94.8 us -> 0 us
  matrix products: 73.3 us -> 0 us
  blocking collectives: 27.5 us -> 0 us
  between operations: 13.8 us -> 0.72 us
    pallas_call x0 -> x3, Pallas kernels: none -> 138 us  [the longest x1 71.5 us: mixed(): pl.pallas_call(mixed_kernel, grid=(experts, 2), out_shape=(jax.ShapeDtype...]
    dot_general x4 -> x0, matrix products: 73.3 us -> none  [the longest x1 22.9 us: local(): jnp.einsum('jwis,jsd->jwid', grad_pair, routed, preferred_element_type=jn...]
    reduce_scatter x2 -> x0, waiting for transfers between devices: 68.3 us -> none  [the longest x1 68.3 us: local(): lax.psum_scatter(partial, 'expert', scatter_dimension=0, tiled=True)]
    all_gather x2 -> x0, blocking collectives: 27.5 us -> none  [the longest x1 20.5 us: local(): ids = lax.all_gather(expert_ids, 'expert', axis=0, tiled=True)]
    all_gather x1 -> x0, waiting for transfers between devices: 26.4 us -> none  [local(): features = lax.all_gather(features, 'expert', axis=0, tiled=True)]
    another operation x1 -> x0, other arithmetic: 3.43 us -> none  [local(): grad_pair = jnp.stack([gate_grad, up_grad], axis=1)]
    convert_element_type x0 -> x3, other arithmetic: none -> 2.59 us  [the longest x1 0.96 us: selector_of(): return (slot.T[:, None, :] == slots[None, :, None]).astype(jnp.bfloat16)]
  transfers between devices with their start and end apart: 3 -> 0, of which waited for: 2 -> 0; matrix products, arithmetic and copies ran while one was open for 13% -> 0% of each run, Pallas kernels for 0% -> 0%
where the time goes in v2:
time: 151 us; the launch traced here: 150 us
  Pallas kernels  138 us (91%)
  other arithmetic  7.11 us (5%)
  local copies, waits for them, and re-layouts  4.18 us (3%)
    pallas_call x1, Pallas kernels, mixed(): pl.pallas_call(mixed_kernel, grid=(experts, 2), out_shape=(jax.ShapeDtype...  71.5 us
    pallas_call x1, Pallas kernels, scatter_sum(): pl.pallas_call(functools.partial(scatter_kernel, groups), out_shape=jax.S...  35.9 us
    pallas_call x1, Pallas kernels, gather_tokens(): pl.pallas_call(functools.partial(gather_kernel, groups), out_shape=jax.Sh...  31.1 us

profile of v2, /device:TPU:9, one launch (start us, length us, event | category | flops | bytes accessed | tf_op | source)
XLA Modules:
  0.0 150.5 jit_solution(16456427334057303976)
XLA Ops:
  0.7 0.7 convert_element_type.21
  1.4 0.1 copy.19
  1.4 0.1 add.27
  1.5 0.1 add.28
  1.6 1.6 %fusion.3 = bf16[32,2176]{1,0:T(8,128)(2,1)} fusion(bf16[32,8]{1,0:T(8,128)(2,1)S(1)} %copy.19, bf16[32,2048]{1,0:T(8,128)(2,1)} %param.4), kind=kLoop, calls=%fused_computation.6 | loop fusion | flops 417792 | bytes 270848 | tf_op jit(solution)/shard_map/concatenate | solution.py:416
  3.2 31.1 %gather_tokens.1 = bf16[2,16,2,16,2176]{4,3,2,1,0:T(8,128)(2,1)} custom-call(bf16[2,16,2176]{2,1,0:T(8,128)(2,1)} %bitcast.26), custom_call_target="tpu_custom_call" | custom-call | tf_op jit(solution)/shard_map/gather_tokens/pallas_call | solution.py:126
  34.2 0.9 fusion.4
  35.2 0.1 copy.14
  35.3 0.1 convert_reduce_fusion
  35.4 0.1 reshape.46
  35.5 0.2 copy.15
  35.7 1.9 %fusion.5 = s32[16,32,4]{2,0,1:T(8,128)S(1)} fusion(s32[16,32,4]{2,0,1:T(8,128)S(1)} %copy.15), kind=kOutput, calls=%fused_computation.14 | output fusion | flops 63488 | bytes 16384 | tf_op jit(solution)/shard_map/jit(cumsum)/reduce_window_sum | solution.py:362
  37.6 0.2 copy.16
  37.8 0.1 reduce_window_sum.14
  37.8 1.0 fusion.chosen
  38.8 0.1 eq.49
  38.9 0.3 copy.18
  39.3 0.9 fusion.1.chosen_back
  40.2 71.5 %expert_pass.1 = (bf16[4,768,128]{2,1,0:T(8,128)(2,1)}, bf16[4,2,768,4096]{3,2,1,0:T(8,128)(2,1)}, bf16[2,512,2048]{2,1,0:T(8,128)(2,1)}) custom-call(bf16[2,512,2176]{2,1,0:T(8,128)(2,1)} %bitcast.24, bf16[4,128,512]{2,1,0:T(8,128)(2,1)} %fusion.chosen, bf16[512,512]{1,0:T(8,128)(2,1)} %fusion.1.chosen_back, bf16[4,2,768,4096]{3,2,1,0:T(8,128)(2,1)} %weights.1, ...), custom_call_target="tpu_custom_call" | custom-call | flops 19327352832 | bytes 100663296 | tf_op jit(solution)/shard_map/expert_pass/pallas_call | solution.py:321
  111.7 0.0 copy-start
  111.8 2.2 %copy-done = bf16[2,512,2048]{2,1,0:T(8,128)(2,1)S(1)} copy-done((bf16[2,512,2048]{2,1,0:T(8,128)(2,1)S(1)}, bf16[2,512,2048]{2,1,0:T(8,128)(2,1)}, u32[]{:S(2)}) %copy-start) | copy-done | bytes 4194328
  113.9 35.9 %scatter_sum.1 = bf16[2,16,2048]{2,1,0:T(8,128)(2,1)S(1)} custom-call(bf16[2,16,2,16,2048]{4,3,2,1,0:T(8,128)(2,1)S(1)} %bitcast.21), custom_call_target="tpu_custom_call" | custom-call | tf_op jit(solution)/shard_map/scatter_sum/pallas_call | solution.py:216
  149.8 0.7 copy.21
  (4 shorter events, 0.0 us)
Async XLA Ops:
  111.7 2.2 %copy-start = (bf16[2,512,2048]{2,1,0:T(8,128)(2,1)S(1)}, bf16[2,512,2048]{2,1,0:T(8,128)(2,1)}, u32[]{:S(2)}) copy-start(bf16[2,512,2048]{2,1,0:T(8,128)(2,1)} %get-tuple-element.8) | copy-start | bytes 12582916

commit v3 on v2

--- a/solution.py
+++ b/solution.py
@@ -149,9 +149,34 @@
     target[...] = total.astype(target.dtype)
 
 
-def scatter_kernel(groups, part, out, one, two, three, four, s1, r1, s2, r2, s3, r3, s4, r4):
+def scatter_kernel(
+    groups, rows, turned, back, weights, out, part, rowgrad, held, one, two, three, four,
+    load, s1, r1, s2, r2, s3, r3, s4, r4,
+):
     me = Place(groups)
     depth = me.depth
+    experts, _, slots, _ = turned.shape
+    chunks, sides, _, width = part.shape
+    half_width = chunks * width
+    half = rows // 2
+    tile = 512 if width % 512 == 0 else 128
+    halves = [pl.ds(0, half), pl.ds(half, half)]
+    f32 = jnp.float32
+
+    def fetch(step):
+        chunk, expert = divmod(step, experts)
+        slot = step % 2
+        return [
+            pltpu.make_async_copy(
+                weights.at[expert, :, :, pl.ds(side * half_width + chunk * width, width)],
+                held.at[slot, side],
+                load.at[slot, side],
+            )
+            for side in range(sides)
+        ]
+
+    for copy in fetch(0):
+        copy.start()
     me.greet()
     other = me.device(core=1 - me.core)
     x_peer, y_peer = me.device(x=1 - me.x), me.device(y=1 - me.y)
@@ -166,87 +191,157 @@
     def arrived(target, sems, at):
         remote(target, target, sems, sems, at, other).wait_recv()
 
-    def side(i, mine):
+    def side_of(i, mine):
         return 1 - mine if i == 0 else mine
 
-    for k in order:
-        for i, j in ((0, 0), (0, 1), (1, 0), (1, 1)):
-            block = me.expert(me.along(k), side(j, me.x), 1 - me.core)
-            source = part.at[side(i, me.y), block]
-            send(source, one.at[k, i, j], s1, r1, (k, i, j), other)
-    for k in order:
-        for i, j in ((0, 0), (0, 1), (1, 0), (1, 1)):
-            arrived(one.at[k, i, j], r1, (k, i, j))
-            block = me.expert(me.along(k), side(j, me.x), me.core)
-            add_into(one.at[k, i, j], part.at[side(i, me.y), block])
-            if i == 0:
-                send(one.at[k, 0, j, 0], two.at[0, k, j], s2, r2, (0, k, j), y_peer)
-            if j == 0:
-                send(one.at[k, i, 0, 1], two.at[1, k, i], s2, r2, (1, k, i), x_peer)
-    for k in order:
-        for j in range(2):
-            arrived(two.at[0, k, j], r2, (0, k, j))
-            add_into(two.at[0, k, j], one.at[k, 1, j, 0])
-            arrived(two.at[1, k, j], r2, (1, k, j))
-            add_into(two.at[1, k, j], one.at[k, j, 1, 1])
-            if j == 0:
-                send(two.at[0, k, 0], three.at[0, k], s3, r3, (0, k), x_peer)
-                send(two.at[1, k, 0], three.at[1, k], s3, r3, (1, k), y_peer)
-    for k in order:
+    def block(c, k, i, j, core):
+        expert = me.expert(me.along(k), side_of(j, me.x), core)
+        at = pl.ds(pl.multiple_of(expert * rows, rows), rows)
+        return part.at[c, side_of(i, me.y), at]
+
+    corners = ((0, 0), (0, 1), (1, 0), (1, 1))
+
+    def to_core(c):
+        for k in order:
+            for i, j in corners:
+                source = block(c, k, i, j, 1 - me.core)
+                send(source, one.at[c, k, i, j], s1, r1, (c, k, i, j), other)
+
+    def to_first(c):
+        for k in order:
+            for i, j in corners:
+                arrived(one.at[c, k, i, j], r1, (c, k, i, j))
+                add_into(one.at[c, k, i, j], block(c, k, i, j, me.core))
+                if i == 0:
+                    source = one.at[c, k, 0, j, halves[0]]
+                    send(source, two.at[c, 0, k, j], s2, r2, (c, 0, k, j), y_peer)
+                if j == 0:
+                    source = one.at[c, k, i, 0, halves[1]]
+                    send(source, two.at[c, 1, k, i], s2, r2, (c, 1, k, i), x_peer)
+
+    def to_second(c):
+        for k in order:
+            for j in range(2):
+                arrived(two.at[c, 0, k, j], r2, (c, 0, k, j))
+                add_into(two.at[c, 0, k, j], one.at[c, k, 1, j, halves[0]])
+                arrived(two.at[c, 1, k, j], r2, (c, 1, k, j))
+                add_into(two.at[c, 1, k, j], one.at[c, k, j, 1, halves[1]])
+                if j == 0:
+                    send(two.at[c, 0, k, 0], three.at[c, 0, k], s3, r3, (c, 0, k), x_peer)
+                    send(two.at[c, 1, k, 0], three.at[c, 1, k], s3, r3, (c, 1, k), y_peer)
+
+    def to_owner(c):
+        for k in order:
+            for h in range(2):
+                arrived(three.at[c, h, k], r3, (c, h, k))
+                add_into(three.at[c, h, k], two.at[c, h, k, 1])
+                if k > 0:
+                    owner = me.device(z=me.along(k))
+                    send(three.at[c, h, k], four.at[c, h, k], s4, r4, (c, h, k), owner)
+
+    def finish(c):
         for h in range(2):
-            arrived(three.at[h, k], r3, (h, k))
-            add_into(three.at[h, k], two.at[h, k, 1])
-            if k > 0:
-                send(three.at[h, k], four.at[h, k], s4, r4, (h, k), me.device(z=me.along(k)))
-    for h in range(2):
-        total = three[h, 0].astype(jnp.float32)
-        for k in range(1, depth):
-            arrived(four.at[h, k], r4, (h, k))
-            total = total + four[h, k].astype(jnp.float32)
-        out[h] = total.astype(out.dtype)
+            total = three[c, h, 0].astype(f32)
+            for k in range(1, depth):
+                arrived(four.at[c, h, k], r4, (c, h, k))
+                total = total + four[c, h, k].astype(f32)
+            out[halves[h], pl.ds(c * width, width)] = total.astype(out.dtype)
+
+    stages = [to_first, to_second, to_owner, finish]
+    waiting = []
+    for step in range(chunks * experts):
+        chunk, expert = divmod(step, experts)
+        slot = step % 2
+        if step + 1 < chunks * experts:
+            for copy in fetch(step + 1):
+                copy.start()
+        for copy in fetch(step):
+            copy.wait()
+        for side in range(sides):
+
+            @pl.loop(0, width // tile)
+            def _(n):
+                at = pl.ds(pl.multiple_of(n * tile, tile), tile)
+                total = jnp.dot(
+                    turned[expert, 0], held[slot, side, 0, :, at], preferred_element_type=f32
+                )
+                total += jnp.dot(
+                    turned[expert, 1], held[slot, side, 1, :, at], preferred_element_type=f32
+                )
+                rowgrad[side, pl.ds(expert * slots, slots), at] = total.astype(rowgrad.dtype)
+
+            if waiting:
+                waiting.pop(0)()
+        if expert == experts - 1:
+            for side in range(sides):
+
+                @pl.loop(0, width // tile)
+                def _(n):
+                    at = pl.ds(pl.multiple_of(n * tile, tile), tile)
+                    part[chunk, side, :, at] = jnp.dot(
+                        back[...], rowgrad[side, :, at], preferred_element_type=f32
+                    ).astype(part.dtype)
+
+            to_core(chunk)
+            waiting += [functools.partial(stage, chunk) for stage in stages]
+    for stage in waiting:
+        stage()
     for copy in started:
         copy.wait_send()
 
 
-def scatter_sum(part):
-    _, groups, halves, rows, width = part.shape
+def scatter_sum(turned, selector, gate_up, groups, rows, half_width, sides):
+    experts, _, units, _ = gate_up.shape
+    slots, tokens = selector.shape[1:]
     depth = groups // 4
+    chunks = 2 if half_width % 256 == 0 else 1
+    width = half_width // chunks
+    bf16 = gate_up.dtype
+    back = jnp.transpose(selector.reshape(experts * slots, tokens))
     dma = pltpu.SemaphoreType.DMA
-    vmem = lambda *lead: pltpu.VMEM(lead + (rows, width), part.dtype)
+    vmem = lambda *dims: pltpu.VMEM(dims + (width,), bf16)
+    whole = pl.BlockSpec(memory_space=pltpu.VMEM)
     return pl.pallas_call(
-        functools.partial(scatter_kernel, groups),
-        out_shape=jax.ShapeDtypeStruct((halves, rows, width), part.dtype),
-        in_specs=[pl.BlockSpec(memory_space=pltpu.VMEM)],
-        out_specs=pl.BlockSpec(memory_space=pltpu.VMEM),
+        functools.partial(scatter_kernel, groups, rows),
+        out_shape=jax.ShapeDtypeStruct((rows, half_width), bf16),
+        in_specs=[whole, whole, pl.BlockSpec(memory_space=pl.ANY)],
+        out_specs=whole,
         scratch_shapes=[
-            vmem(depth, 2, 2, 2),
-            vmem(2, depth, 2),
-            vmem(2, depth),
-            vmem(2, depth),
-            dma((depth, 2, 2)),
-            dma((depth, 2, 2)),
-            dma((2, depth, 2)),
-            dma((2, depth, 2)),
-            dma((2, depth)),
-            dma((2, depth)),
-            dma((2, depth)),
-            dma((2, depth)),
+            vmem(chunks, sides, tokens),
+            vmem(sides, experts * slots),
+            vmem(2, sides, 2, units),
+            vmem(chunks, depth, 2, 2, rows),
+            vmem(chunks, 2, depth, 2, rows // 2),
+            vmem(chunks, 2, depth, rows // 2),
+            vmem(chunks, 2, depth, rows // 2),
+            dma((2, sides)),
+            dma((chunks, depth, 2, 2)),
+            dma((chunks, depth, 2, 2)),
+            dma((chunks, 2, depth, 2)),
+            dma((chunks, 2, depth, 2)),
+            dma((chunks, 2, depth)),
+            dma((chunks, 2, depth)),
+            dma((chunks, 2, depth)),
+            dma((chunks, 2, depth)),
         ],
         compiler_params=pltpu.CompilerParams(
-            collective_id=1, has_side_effects=True, vmem_limit_bytes=24 * MIB
+            collective_id=1, has_side_effects=True, vmem_limit_bytes=58 * MIB
         ),
-        name="scatter_sum",
-    )(part)
+        cost_estimate=pl.CostEstimate(
+            flops=2 * gate_up.size * slots, bytes_accessed=2 * gate_up.size, transcendentals=0
+        ),
+        name="row_gradient",
+    )(turned, back, gate_up)
 
 
 def mixed_kernel(
-    features, chosen, chosen_back, weights, grad, hidden, weight_grad, summed, routed, parts, pair, turned
+    features, chosen, weights, grad, hidden, weight_grad, turned, routed, pair
 ):
-    expert, turn = pl.program_id(0), pl.program_id(1)
-    sides, _, half = features.shape
-    units, slots = pair.shape[1:]
+    turn = pl.program_id(1)
+    sides = features.shape[0]
+    units = pair.shape[1]
     width = routed.shape[1]
-    half_width = summed.shape[2]
+    half_width = width // sides
     tile = 512 if half_width % 512 == 0 else 128
     rows = 256 if units % 256 == 0 else 16
     f32 = jnp.float32
@@ -286,37 +381,18 @@
             pair[turn], routed[:, at], preferred_element_type=f32
         ).astype(weight_grad.dtype)
 
-    @pl.when(turn == 1)
+    @pl.when(turn == 0)
     def _():
-        turned[0] = pair[0].T
-        turned[1] = pair[1].T
-
-        @pl.loop(0, width // tile)
-        def _(n):
-            at = pl.ds(pl.multiple_of(n * tile, tile), tile)
-            total = jnp.dot(turned[0], weights[0, 0, :, at], preferred_element_type=f32)
-            total += jnp.dot(turned[1], weights[0, 1, :, at], preferred_element_type=f32)
-            parts[pl.ds(pl.multiple_of(expert * slots, slots), slots), at] = total.astype(parts.dtype)
-
-    @pl.when((turn == 1) & (expert == pl.num_programs(0) - 1))
-    def _():
-        @pl.loop(0, half_width // tile)
-        def _(n):
-            at = pl.ds(pl.multiple_of(n * tile, tile), tile)
-            for side in range(sides):
-                come = pl.ds(pl.multiple_of(side * half_width + n * tile, tile), tile)
-                summed[side, :, at] = jnp.dot(
-                    chosen_back[...], parts[:, come], preferred_element_type=f32
-                ).astype(summed.dtype)
-
-
-def mixed(features, selector, gate_up, hidden_grad, half_width):
+        turned[0, 0] = pair[0].T
+        turned[0, 1] = pair[1].T
+
+
+def mixed(features, selector, gate_up, hidden_grad):
     experts, _, units, width = gate_up.shape
     slots = hidden_grad.shape[2]
     sides, tokens, _ = features.shape
-    back = jnp.transpose(selector.reshape(experts * slots, tokens))
     bf16 = gate_up.dtype
-    flops = 2 * experts * units * width * slots * 6
+    flops = 2 * experts * units * width * slots * 4
     whole = pl.BlockSpec(memory_space=pltpu.VMEM)
     return pl.pallas_call(
         mixed_kernel,
@@ -324,25 +400,22 @@
         out_shape=(
             jax.ShapeDtypeStruct(hidden_grad.shape, bf16),
             jax.ShapeDtypeStruct(gate_up.shape, bf16),
-            jax.ShapeDtypeStruct((sides, tokens, half_width), bf16),
+            jax.ShapeDtypeStruct((experts, 2, slots, units), bf16),
         ),
         in_specs=[
             whole,
             pl.BlockSpec((1, slots, tokens), lambda j, p: (j, 0, 0)),
-            whole,
             pl.BlockSpec((1, 2, units, width), lambda j, p: (j, 0, 0, 0)),
             pl.BlockSpec((1, units, slots), lambda j, p: (j, 0, 0)),
         ],
         out_specs=(
             pl.BlockSpec((1, units, slots), lambda j, p: (j, 0, 0)),
             pl.BlockSpec((1, 1, units, width), lambda j, p: (j, p, 0, 0)),
-            whole,
+            pl.BlockSpec((1, 2, slots, units), lambda j, p: (j, 0, 0, 0)),
         ),
         scratch_shapes=[
             pltpu.VMEM((slots, width), bf16),
-            pltpu.VMEM((experts * slots, width), bf16),
             pltpu.VMEM((2, units, slots), bf16),
-            pltpu.VMEM((2, slots, units), bf16),
         ],
         compiler_params=pltpu.CompilerParams(
             dimension_semantics=("arbitrary", "arbitrary"), vmem_limit_bytes=60 * MIB
@@ -351,7 +424,7 @@
             flops=flops, bytes_accessed=4 * gate_up.size, transcendentals=experts * units * slots
         ),
         name="expert_pass",
-    )(features, selector, back, gate_up, hidden_grad)
+    )(features, selector, gate_up, hidden_grad)
 
 
 def selector_of(ids, first, local_experts, groups, capacity):
@@ -419,9 +492,9 @@
     selector = selector_of(
         ids, lax.axis_index("expert") * local_experts, local_experts, groups, capacity
     )
-    hidden, weight_grad, partial = mixed(full, selector, gate_up, hidden_grad, width)
-    token_grad = scatter_sum(partial.reshape(fsdp, groups, 2, rows // 2, width))
-    return (hidden, weight_grad, token_grad.reshape(rows, width))
+    hidden, weight_grad, turned = mixed(full, selector, gate_up, hidden_grad)
+    token_grad = scatter_sum(turned, selector, gate_up, groups, rows, width, fsdp)
+    return (hidden, weight_grad, token_grad)
 
 
 def fits(mesh, gate_up_shape, ids_shape, tokens_shape):

time: 151 us -> 174 us (1.15)
  Pallas kernels: 138 us -> 163 us
    pallas_call x1, Pallas kernels: 35.9 us -> 59.4 us  [scatter_sum(): pl.pallas_call(functools.partial(scatter_kernel, groups, rows), out_shape...]
where the time goes in v3:
time: 174 us; the launch traced here: 173 us
  Pallas kernels  163 us (94%)
  other arithmetic  7.05 us (4%)
  local copies, waits for them, and re-layouts  2.92 us (2%)
    pallas_call x1, Pallas kernels, mixed(): pl.pallas_call(mixed_kernel, grid=(experts, 2), out_shape=(jax.ShapeDtype...  72 us
    pallas_call x1, Pallas kernels, scatter_sum(): pl.pallas_call(functools.partial(scatter_kernel, groups, rows), out_shape...  59.4 us
    pallas_call x1, Pallas kernels, gather_tokens(): pl.pallas_call(functools.partial(gather_kernel, groups), out_shape=jax.Sh...  31.1 us

profile of v3, /device:TPU:9, one launch (start us, length us, event | category | flops | bytes accessed | tf_op | source)
XLA Modules:
  0.0 173.2 jit_solution(12186937782813789293)
XLA Ops:
  0.6 0.7 convert_element_type.21
  1.3 0.1 copy.19
  1.4 1.6 fusion.3
  3.0 31.1 %gather_tokens.1 = bf16[2,16,2,16,2176]{4,3,2,1,0:T(8,128)(2,1)} custom-call(bf16[2,16,2176]{2,1,0:T(8,128)(2,1)} %bitcast.22), custom_call_target="tpu_custom_call" | custom-call | tf_op jit(solution)/shard_map/gather_tokens/pallas_call | solution.py:126
  34.1 0.9 fusion.4
  35.0 0.1 copy.14
  35.1 0.1 convert_reduce_fusion
  35.2 0.1 reshape.40
  35.3 0.2 copy.15
  35.5 1.9 %fusion.5 = s32[16,32,4]{2,0,1:T(8,128)S(1)} fusion(s32[16,32,4]{2,0,1:T(8,128)S(1)} %copy.15), kind=kOutput, calls=%fused_computation.14 | output fusion | flops 63488 | bytes 16384 | tf_op jit(solution)/shard_map/jit(cumsum)/reduce_window_sum | solution.py:435
  37.4 0.2 copy.16
  37.6 0.1 reduce_window_sum.14
  37.7 0.1 add.27
  37.7 0.1 add.28
  37.8 0.9 fusion.chosen
  38.8 72.0 %expert_pass.1 = (bf16[4,768,128]{2,1,0:T(8,128)(2,1)}, bf16[4,2,768,4096]{3,2,1,0:T(8,128)(2,1)}, bf16[4,2,128,768]{3,2,1,0:T(8,128)(2,1)}) custom-call(bf16[2,512,2176]{2,1,0:T(8,128)(2,1)} %bitcast.20, bf16[4,128,512]{2,1,0:T(8,128)(2,1)} %fusion.chosen, bf16[4,2,768,4096]{3,2,1,0:T(8,128)(2,1)} %weights.3, bf16[4,768,128]{2,1,0:T(8,128)(2,1)} %grad.1), custom_call_target="tpu_custom_call" | custom-call | flops 12884901888 | bytes 100663296 | tf_op jit(solution)/shard_map/expert_pass/pallas_call | solution.py:397
  110.8 0.1 eq.49
  110.9 0.3 copy.18
  111.3 0.9 fusion.1.back
  112.2 59.4 %row_gradient.1 = bf16[32,2048]{1,0:T(8,128)(2,1)} custom-call(bf16[4,2,128,768]{3,2,1,0:T(8,128)(2,1)} %get-tuple-element.8.turned, bf16[512,512]{1,0:T(8,128)(2,1)} %fusion.1.back, bf16[4,2,768,4096]{3,2,1,0:T(8,128)(2,1)} %weights.3), custom_call_target="tpu_custom_call" | custom-call | flops 6442450944 | bytes 50331648 | tf_op jit(solution)/shard_map/row_gradient/pallas_call | solution.py:304
  171.6 1.6 copy.21
  (4 shorter events, 0.0 us)

commit v4 on v2

--- a/solution.py
+++ b/solution.py
@@ -240,15 +240,14 @@
 
 
 def mixed_kernel(
-    features, chosen, chosen_back, weights, grad, hidden, weight_grad, summed, routed, parts, pair, turned
+    features, chosen, chosen_back, weights, grad, hidden, weight_grad, summed, routed, parts, pair, total
 ):
     expert, turn = pl.program_id(0), pl.program_id(1)
-    sides, _, half = features.shape
-    units, slots = pair.shape[1:]
-    width = routed.shape[1]
+    last = pl.num_programs(1) - 1
+    sides = features.shape[0]
+    slots, width = routed.shape
     half_width = summed.shape[2]
     tile = 512 if half_width % 512 == 0 else 128
-    rows = 256 if units % 256 == 0 else 16
     f32 = jnp.float32
 
     @pl.when(turn == 0)
@@ -262,43 +261,36 @@
                     chosen[0], features[side, :, at], preferred_element_type=f32
                 ).astype(routed.dtype)
 
-        @pl.loop(0, units // rows)
-        def _(n):
-            at = pl.ds(pl.multiple_of(n * rows, rows), rows)
-            contract = (((1,), (1,)), ((), ()))
-            gate = lax.dot_general(
-                weights[0, 0, at, :], routed[...], contract, preferred_element_type=f32
-            )
-            up = lax.dot_general(
-                weights[0, 1, at, :], routed[...], contract, preferred_element_type=f32
-            )
-            sigmoid = 1.0 / (1.0 + jnp.exp(-gate))
-            active = gate * sigmoid
-            hidden[0, at, :] = (active * up).astype(hidden.dtype)
-            slope = grad[0, at, :].astype(f32)
-            pair[0, at, :] = (slope * up * sigmoid * (1.0 + gate * (1.0 - sigmoid))).astype(pair.dtype)
-            pair[1, at, :] = (slope * active).astype(pair.dtype)
+        total[...] = jnp.zeros_like(total)
+
+    contract = (((1,), (1,)), ((), ()))
+    gate = lax.dot_general(weights[0, 0], routed[...], contract, preferred_element_type=f32)
+    up = lax.dot_general(weights[0, 1], routed[...], contract, preferred_element_type=f32)
+    sigmoid = 1.0 / (1.0 + jnp.exp(-gate))
+    active = gate * sigmoid
+    hidden[0] = (active * up).astype(hidden.dtype)
+    slope = grad[0].astype(f32)
+    pair[0] = (slope * up * sigmoid * (1.0 + gate * (1.0 - sigmoid))).astype(pair.dtype)
+    pair[1] = (slope * active).astype(pair.dtype)
+    turned = [pair[0].T, pair[1].T]
 
     @pl.loop(0, width // tile)
     def _(n):
         at = pl.ds(pl.multiple_of(n * tile, tile), tile)
-        weight_grad[0, 0, :, at] = jnp.dot(
-            pair[turn], routed[:, at], preferred_element_type=f32
-        ).astype(weight_grad.dtype)
-
-    @pl.when(turn == 1)
+        for w in range(2):
+            weight_grad[0, w, :, at] = jnp.dot(
+                pair[w], routed[:, at], preferred_element_type=f32
+            ).astype(weight_grad.dtype)
+        rows = jnp.dot(turned[0], weights[0, 0, :, at], preferred_element_type=f32)
+        rows += jnp.dot(turned[1], weights[0, 1, :, at], preferred_element_type=f32)
+        total[:, at] += rows
+
+    @pl.when(turn == last)
     def _():
-        turned[0] = pair[0].T
-        turned[1] = pair[1].T
-
-        @pl.loop(0, width // tile)
-        def _(n):
-            at = pl.ds(pl.multiple_of(n * tile, tile), tile)
-            total = jnp.dot(turned[0], weights[0, 0, :, at], preferred_element_type=f32)
-            total += jnp.dot(turned[1], weights[0, 1, :, at], preferred_element_type=f32)
-            parts[pl.ds(pl.multiple_of(expert * slots, slots), slots), at] = total.astype(parts.dtype)
-
-    @pl.when((turn == 1) & (expert == pl.num_programs(0) - 1))
+        at = pl.ds(pl.multiple_of(expert * slots, slots), slots)
+        parts[at, :] = total[...].astype(parts.dtype)
+
+    @pl.when((turn == last) & (expert == pl.num_programs(0) - 1))
     def _():
         @pl.loop(0, half_width // tile)
         def _(n):
@@ -316,11 +308,12 @@
     sides, tokens, _ = features.shape
     back = jnp.transpose(selector.reshape(experts * slots, tokens))
     bf16 = gate_up.dtype
+    rows = 256 if units % 256 == 0 else 16
     flops = 2 * experts * units * width * slots * 6
     whole = pl.BlockSpec(memory_space=pltpu.VMEM)
     return pl.pallas_call(
         mixed_kernel,
-        grid=(experts, 2),
+        grid=(experts, units // rows),
         out_shape=(
             jax.ShapeDtypeStruct(hidden_grad.shape, bf16),
             jax.ShapeDtypeStruct(gate_up.shape, bf16),
@@ -330,19 +323,19 @@
             whole,
             pl.BlockSpec((1, slots, tokens), lambda j, p: (j, 0, 0)),
             whole,
-            pl.BlockSpec((1, 2, units, width), lambda j, p: (j, 0, 0, 0)),
-            pl.BlockSpec((1, units, slots), lambda j, p: (j, 0, 0)),
+            pl.BlockSpec((1, 2, rows, width), lambda j, p: (j, 0, p, 0)),
+            pl.BlockSpec((1, rows, slots), lambda j, p: (j, p, 0)),
         ],
         out_specs=(
-            pl.BlockSpec((1, units, slots), lambda j, p: (j, 0, 0)),
-            pl.BlockSpec((1, 1, units, width), lambda j, p: (j, p, 0, 0)),
+            pl.BlockSpec((1, rows, slots), lambda j, p: (j, p, 0)),
+            pl.BlockSpec((1, 2, rows, width), lambda j, p: (j, 0, p, 0)),
             whole,
         ),
         scratch_shapes=[
             pltpu.VMEM((slots, width), bf16),
             pltpu.VMEM((experts * slots, width), bf16),
-            pltpu.VMEM((2, units, slots), bf16),
-            pltpu.VMEM((2, slots, units), bf16),
+            pltpu.VMEM((2, rows, slots), bf16),
+            pltpu.VMEM((slots, width), jnp.float32),
         ],
         compiler_params=pltpu.CompilerParams(
             dimension_semantics=("arbitrary", "arbitrary"), vmem_limit_bytes=60 * MIB

time: 151 us -> 146 us (0.967)
  Pallas kernels: 138 us -> 134 us
    pallas_call x1, Pallas kernels: 71.5 us -> 67 us  [mixed(): pl.pallas_call(mixed_kernel, grid=(experts, units // rows), out_shape=(ja...]
where the time goes in v4:
time: 146 us
  Pallas kernels  134 us (92%)
  other arithmetic  7.11 us (5%)
  local copies, waits for them, and re-layouts  4.18 us (3%)
    pallas_call x1, Pallas kernels, mixed(): pl.pallas_call(mixed_kernel, grid=(experts, units // rows), out_shape=(ja...  67 us
    pallas_call x1, Pallas kernels, scatter_sum(): pl.pallas_call(functools.partial(scatter_kernel, groups), out_shape=jax.S...  35.9 us
    pallas_call x1, Pallas kernels, gather_tokens(): pl.pallas_call(functools.partial(gather_kernel, groups), out_shape=jax.Sh...  31.1 us
    unnamed x4, local copies, waits for them, and re-layouts  2.93 us

profile of v4, /device:TPU:9, one launch (start us, length us, event | category | flops | bytes accessed | tf_op | source)
XLA Modules:
  0.0 145.9 jit_solution(12893605744677331988)
XLA Ops:
  0.7 0.7 convert_element_type.21
  1.4 0.1 copy.19
  1.4 0.1 add.27
  1.5 0.1 add.28
  1.6 1.6 %fusion.3 = bf16[32,2176]{1,0:T(8,128)(2,1)} fusion(bf16[32,8]{1,0:T(8,128)(2,1)S(1)} %copy.19, bf16[32,2048]{1,0:T(8,128)(2,1)} %param.4), kind=kLoop, calls=%fused_computation.6 | loop fusion | flops 417792 | bytes 270848 | tf_op jit(solution)/shard_map/concatenate | solution.py:409
  3.2 31.1 %gather_tokens.1 = bf16[2,16,2,16,2176]{4,3,2,1,0:T(8,128)(2,1)} custom-call(bf16[2,16,2176]{2,1,0:T(8,128)(2,1)} %bitcast.26), custom_call_target="tpu_custom_call" | custom-call | tf_op jit(solution)/shard_map/gather_tokens/pallas_call | solution.py:126
  34.2 0.9 fusion.4
  35.2 0.1 copy.14
  35.3 0.1 convert_reduce_fusion
  35.4 0.1 reshape.46
  35.5 0.2 copy.15
  35.7 1.9 %fusion.5 = s32[16,32,4]{2,0,1:T(8,128)S(1)} fusion(s32[16,32,4]{2,0,1:T(8,128)S(1)} %copy.15), kind=kOutput, calls=%fused_computation.14 | output fusion | flops 63488 | bytes 16384 | tf_op jit(solution)/shard_map/jit(cumsum)/reduce_window_sum | solution.py:355
  37.6 0.2 copy.16
  37.8 0.1 reduce_window_sum.14
  37.8 1.0 fusion.chosen
  38.8 0.1 eq.49
  38.9 0.3 copy.18
  39.3 0.9 fusion.1.chosen_back
  40.2 67.0 %expert_pass.1 = (bf16[4,768,128]{2,1,0:T(8,128)(2,1)}, bf16[4,2,768,4096]{3,2,1,0:T(8,128)(2,1)}, bf16[2,512,2048]{2,1,0:T(8,128)(2,1)}) custom-call(bf16[2,512,2176]{2,1,0:T(8,128)(2,1)} %bitcast.24, bf16[4,128,512]{2,1,0:T(8,128)(2,1)} %fusion.chosen, bf16[512,512]{1,0:T(8,128)(2,1)} %fusion.1.chosen_back, bf16[4,2,768,4096]{3,2,1,0:T(8,128)(2,1)} %weights.1, ...), custom_call_target="tpu_custom_call" | custom-call | flops 19327352832 | bytes 100663296 | tf_op jit(solution)/shard_map/expert_pass/pallas_call | solution.py:314
  107.2 0.0 copy-start
  107.2 2.2 %copy-done = bf16[2,512,2048]{2,1,0:T(8,128)(2,1)S(1)} copy-done((bf16[2,512,2048]{2,1,0:T(8,128)(2,1)S(1)}, bf16[2,512,2048]{2,1,0:T(8,128)(2,1)}, u32[]{:S(2)}) %copy-start) | copy-done | bytes 4194328
  109.4 35.9 %scatter_sum.1 = bf16[2,16,2048]{2,1,0:T(8,128)(2,1)S(1)} custom-call(bf16[2,16,2,16,2048]{4,3,2,1,0:T(8,128)(2,1)S(1)} %bitcast.21), custom_call_target="tpu_custom_call" | custom-call | tf_op jit(solution)/shard_map/scatter_sum/pallas_call | solution.py:216
  145.3 0.7 copy.21
  (4 shorter events, 0.0 us)
Async XLA Ops:
  107.2 2.2 %copy-start = (bf16[2,512,2048]{2,1,0:T(8,128)(2,1)S(1)}, bf16[2,512,2048]{2,1,0:T(8,128)(2,1)}, u32[]{:S(2)}) copy-start(bf16[2,512,2048]{2,1,0:T(8,128)(2,1)} %get-tuple-element.8) | copy-start | bytes 12582916
